TPU v7x, 32 devices: a whole 2x2x4 slice. The times are simulated.
32 devices in a mesh: dp: 8 (over z, x), head: 4 (over y, core).
Axes of the slice: x: 2, y: 2, z: 4, core: 2. Of those that a mesh axis runs over, the one named last changes fastest.
Arguments:
- tokens: bfloat16 [64, 512, 768], P('dp', 'head'), may hold values from -8 to 8
- segment_labels: int32 [64, 512], P('dp'), may hold values from 0 to 3, as said below
- joint_projection: bfloat16 [768, 2304], replicated, may hold values from -0.21875 to 0.21875
- output_projection: bfloat16 [768, 768], replicated, may hold values from -0.625 to 0.625
- first_gain: float32 [768], replicated, may hold values from 0.1 to 1.9
- first_offset: float32 [768], replicated, may hold values from -1.75 to 1.75
- expand_weight: bfloat16 [768, 6144], replicated, may hold values from -0.21875 to 0.21875
- reduce_weight: bfloat16 [3072, 768], replicated, may hold values from -0.15625 to 0.15625
- second_gain: float32 [768], replicated, may hold values from 0.1 to 1.9
- second_offset: float32 [768], replicated, may hold values from -1.75 to 1.75
- cotangent: bfloat16 [64, 512, 768], P('dp', 'head'), may hold values from -8 to 8
Outputs:
- layer_output: bfloat16 [64, 512, 768], P('dp', 'head')
- tokens_gradient: bfloat16 [64, 512, 768], P('dp', 'head')
- joint_gradient: float32 [768, 2304], P('dp')
- projection_gradient: float32 [768, 768], P('dp')
- first_gain_gradient: float32 [768], P('dp')
- first_offset_gradient: float32 [768], P('dp')
- expand_gradient: float32 [768, 6144], P('dp')
- reduce_gradient: float32 [3072, 768], P('dp')
- second_gain_gradient: float32 [768], P('dp')
- second_offset_gradient: float32 [768], P('dp')
Inputs may be any that keep to these rules, and one draw needn't show every extreme that they name: `segment_labels`: in every row the labels never fall and take each value from 0 to 3; label 1 covers every position from 64 up to 447.
All inputs are finite; a program needn't handle non-finite values.
Results may differ from a plain program's by a relative error of at most 0.015.
Values may be sent and summed in bfloat16 or wider, within the bound.
No kernel may reach another device: no remote copies, remote signals or barrier semaphores. Data moves between devices by JAX's collectives and lax.ppermute only.
A program may use at most 256 MiB of HBM per device.

v0:
```python
import math

import jax
import jax.numpy as jnp
import numpy as np
from jax import lax
from jax.sharding import PartitionSpec as P

H = 12
DH = 64


EPSILON = 1e-12
NEG_FILL = -1e30


def head_slopes(heads_total):
    closest = 2 ** int(math.floor(math.log2(heads_total)))

    def power_slopes(number):
        first_slope = 2.0 ** (-8.0 / number)
        return [first_slope ** (counter + 1) for counter in range(number)]

    listed = power_slopes(closest)
    listed = listed + power_slopes(2 * closest)[0::2][: heads_total - closest]
    return np.array(listed, dtype=np.float32)


def layer_norm(values, gain, offset):
    center = values - jnp.mean(values, axis=-1, keepdims=True)
    spread = jnp.mean(center * center, axis=-1, keepdims=True)
    return center * lax.rsqrt(spread + EPSILON) * gain + offset


def gated_unit(gate_up):
    half_width = gate_up.shape[-1] // 2
    return jax.nn.gelu(gate_up[:, :half_width], approximate=False) * gate_up[:, half_width:]


def masked_scores(queries, keys_block, labels, slopes):
    length = queries.shape[1]
    raw_scores = jnp.einsum(
        "rqhd,rkhd->rhqk", queries, keys_block, preferred_element_type=jnp.float32
    )
    places = jnp.arange(length)
    distance = jnp.abs(places[:, None] - places[None, :]).astype(jnp.float32)
    scores = (
        raw_scores * queries.shape[-1] ** (-0.5)
        - slopes[None, :, None, None] * distance[None, None]
    )
    matching = labels[:, None, :, None] == labels[:, None, None, :]
    return jnp.where(matching, scores, NEG_FILL)


def attend_forward(queries, keys_block, values_block, labels, slopes):
    masked = masked_scores(queries, keys_block, labels, slopes)
    row_top = jnp.max(masked, axis=-1, keepdims=True)
    exponent = jnp.exp(masked - row_top)
    row_total = jnp.sum(exponent, axis=-1, keepdims=True)
    probability = (exponent / row_total).astype(jnp.bfloat16)
    attended = jnp.einsum(
        "rhqk,rkhd->rqhd", probability, values_block, preferred_element_type=jnp.float32
    )
    return (attended, row_top + jnp.log(row_total))


def attend_backward(queries, keys_block, values_block, labels, slopes, log_total, back_out):
    masked = masked_scores(queries, keys_block, labels, slopes)
    probability = jnp.exp(masked - log_total)
    back_probs = jnp.einsum(
        "rqhd,rkhd->rhqk", back_out, values_block, preferred_element_type=jnp.float32
    )
    inner = jnp.sum(probability * back_probs, axis=-1, keepdims=True)
    back_scores = (probability * (back_probs - inner)).astype(jnp.bfloat16)
    score_scale = queries.shape[-1] ** (-0.5)
    back_queries = (
        jnp.einsum("rhqk,rkhd->rqhd", back_scores, keys_block, preferred_element_type=jnp.float32)
        * score_scale
    )
    back_keys = (
        jnp.einsum("rhqk,rqhd->rkhd", back_scores, queries, preferred_element_type=jnp.float32)
        * score_scale
    )
    back_values = jnp.einsum(
        "rhqk,rqhd->rkhd",
        probability.astype(jnp.bfloat16),
        back_out,
        preferred_element_type=jnp.float32,
    )
    return (back_queries, back_keys, back_values)


def local(
    tokens,
    segment_labels,
    joint_projection,
    output_projection,
    first_gain,
    first_offset,
    expand_weight,
    reduce_weight,
    second_gain,
    second_offset,
    cotangent,
):
    row_count, quarter, model_width = tokens.shape
    length = segment_labels.shape[1]
    groups_count = lax.axis_size("head")
    group_index = lax.axis_index("head")
    group_heads = H // groups_count
    group_width = group_heads * DH
    slopes = lax.dynamic_slice_in_dim(
        jnp.asarray(head_slopes(H), dtype=jnp.float32), group_index * group_heads, group_heads
    )
    flat_tokens = tokens.reshape(-1, model_width)
    joint_local = jnp.dot(flat_tokens, joint_projection, preferred_element_type=jnp.float32).astype(
        jnp.bfloat16
    )
    joint_heads = lax.all_to_all(
        joint_local.reshape(row_count, quarter, 3, groups_count, group_width),
        "head",
        split_axis=3,
        concat_axis=1,
        tiled=True,
    )
    joint_heads = joint_heads.reshape(row_count, length, 3, group_heads, DH)
    queries = joint_heads[:, :, 0]
    keys_block = joint_heads[:, :, 1]
    values_block = joint_heads[:, :, 2]
    attended, log_total = attend_forward(queries, keys_block, values_block, segment_labels, slopes)
    attended_low = attended.astype(jnp.bfloat16).reshape(row_count, length, group_width)
    token_heads = lax.all_to_all(
        attended_low.reshape(row_count, length, 1, group_width),
        "head",
        split_axis=1,
        concat_axis=2,
        tiled=True,
    )
    token_heads = token_heads.reshape(-1, model_width)
    branch = jnp.dot(token_heads, output_projection, preferred_element_type=jnp.float32)
    hidden, first_norm_back = jax.vjp(
        layer_norm, flat_tokens.astype(jnp.float32) + branch, first_gain, first_offset
    )
    hidden_low = hidden.astype(jnp.bfloat16)
    gate_up = jnp.dot(hidden_low, expand_weight, preferred_element_type=jnp.float32)
    active, gated_back = jax.vjp(gated_unit, gate_up)
    active_low = active.astype(jnp.bfloat16)
    mixed = jnp.dot(active_low, reduce_weight, preferred_element_type=jnp.float32)
    output, second_norm_back = jax.vjp(layer_norm, hidden + mixed, second_gain, second_offset)
    layer_output = output.astype(jnp.bfloat16).reshape(tokens.shape)
    back_two, second_gain_back, second_offset_back = second_norm_back(
        cotangent.reshape(-1, model_width).astype(jnp.float32)
    )
    back_mixed = back_two.astype(jnp.bfloat16)
    reduce_back = jnp.dot(active_low.T, back_mixed, preferred_element_type=jnp.float32)
    (back_gate_up,) = gated_back(
        jnp.dot(back_mixed, reduce_weight.T, preferred_element_type=jnp.float32)
    )
    back_gate_up = back_gate_up.astype(jnp.bfloat16)
    expand_back = jnp.dot(hidden_low.T, back_gate_up, preferred_element_type=jnp.float32)
    back_hidden = back_two + jnp.dot(
        back_gate_up, expand_weight.T, preferred_element_type=jnp.float32
    )
    back_one, first_gain_back, first_offset_back = first_norm_back(back_hidden)
    back_branch = back_one.astype(jnp.bfloat16)
    projection_back = jnp.dot(token_heads.T, back_branch, preferred_element_type=jnp.float32)
    back_tokens_heads = jnp.dot(
        back_branch, output_projection.T, preferred_element_type=jnp.float32
    ).astype(jnp.bfloat16)
    back_attended = lax.all_to_all(
        back_tokens_heads.reshape(row_count, quarter, groups_count, group_width),
        "head",
        split_axis=2,
        concat_axis=1,
        tiled=True,
    )
    back_attended = back_attended.reshape(row_count, length, group_heads, DH)
    back_queries, back_keys, back_values = attend_backward(
        queries, keys_block, values_block, segment_labels, slopes, log_total, back_attended
    )
    back_joint = jnp.stack((back_queries, back_keys, back_values), axis=2).astype(jnp.bfloat16)
    back_joint_tokens = lax.all_to_all(
        back_joint.reshape(row_count, length, 3, 1, group_width),
        "head",
        split_axis=1,
        concat_axis=3,
        tiled=True,
    )
    back_joint_tokens = back_joint_tokens.reshape(-1, 3 * model_width)
    joint_back = jnp.dot(flat_tokens.T, back_joint_tokens, preferred_element_type=jnp.float32)
    tokens_back = back_one + jnp.dot(
        back_joint_tokens, joint_projection.T, preferred_element_type=jnp.float32
    )
    tokens_gradient = tokens_back.astype(jnp.bfloat16).reshape(tokens.shape)
    summed = (
        lax.psum_scatter(joint_back, "dp", scatter_dimension=0, tiled=True),
        lax.psum_scatter(projection_back, "dp", scatter_dimension=0, tiled=True),
        lax.psum_scatter(first_gain_back, "dp", scatter_dimension=0, tiled=True),
        lax.psum_scatter(first_offset_back, "dp", scatter_dimension=0, tiled=True),
        lax.psum_scatter(expand_back, "dp", scatter_dimension=0, tiled=True),
        lax.psum_scatter(reduce_back, "dp", scatter_dimension=0, tiled=True),
        lax.psum_scatter(second_gain_back, "dp", scatter_dimension=0, tiled=True),
        lax.psum_scatter(second_offset_back, "dp", scatter_dimension=0, tiled=True),
    )
    summed = lax.psum(
        (summed[0], summed[1], summed[2], summed[3], summed[4], summed[5], summed[6], summed[7]),
        "head",
    )
    return (
        layer_output,
        tokens_gradient,
        summed[0],
        summed[1],
        summed[2],
        summed[3],
        summed[4],
        summed[5],
        summed[6],
        summed[7],
    )


def solution(mesh):
    placed = (
        P("dp", "head", None),
        P("dp", None),
        P(),
        P(),
        P(),
        P(),
        P(),
        P(),
        P(),
        P(),
        P("dp", "head", None),
    )
    return jax.shard_map(
        local,
        mesh=mesh,
        in_specs=placed,
        out_specs=(
            P("dp", "head", None),
            P("dp", "head", None),
            P("dp", None),
            P("dp", None),
            P("dp"),
            P("dp"),
            P("dp", None),
            P("dp", None),
            P("dp"),
            P("dp"),
        ),
        check_vma=False,
    )
```

profile of v0, /device:TPU:0, one launch (start us, length us, event | category | flops | bytes accessed | tf_op | source)
XLA Modules:
  0.0 1343.5 jit_solution(5275799313649806991)
XLA Ops:
  9.2 7.4 convolution_convert_fusion
  16.6 12.8 reshape.217
  29.4 8.2 copy.71
  48.4 49.1 %all-to-all-done = bf16[8,128,3,4,192]{1,0,4,2,3:T(8,128)(2,1)} async-done(((bf16[8,128,3,4,192]{1,0,4,2,3:T(8,128)(2,1)}), bf16[8,128,3,4,192]{1,0,4,2,3:T(8,128)(2,1)}, u32[]{:S(2)}, u32[]{:S(2)}) %all-to-all-start) | async-done | bytes 4718624 | tf_op jit(solution)/shard_map/all_to_all | solution.py:119
  97.5 8.2 copy.72
  105.7 8.1 reshape.209
  113.8 14.4 %fusion.50 = (f32[8,3,512]{2,1,0:T(4,128)S(1)}, f32[8,3,512,512]{2,3,1,0:T(8,128)}) fusion(f32[3,512,512]{1,2,0:T(8,128)} %broadcast_multiply_fusion, bf16[8,512,3,3,64]{1,4,3,0,2:T(8,128)(2,1)} %reshape.209, pred[8,512,512]{1,2,0:T(8,128)(4,1)} %broadcast_compare_fusion), kind=kOutput, calls=%fused_computation.98 | convolution fusion | flops 830459904 | bytes 33603584 | tf_op jit(solution)/shard_map/rqhd,rkhd->rhqk/dot_general | solution.py:42
  128.2 10.4 fusion
  138.7 11.9 fusion.28
  154.9 30.4 %all_to_all.60 = bf16[8,512,1,192]{3,0,2,1:T(8,128)(2,1)} all-to-all(bf16[8,512,1,192]{3,0,2,1:T(8,128)(2,1)} %copy.74), channel_id=1, replica_groups=mesh['dp'=8,'head'=4] {'head'}, dimensions={1} | all-to-all | bytes 3145728 | tf_op jit(solution)/shard_map/all_to_all | solution.py:132
  195.9 17.9 %fusion.45 = f32[1024,6144]{1,0:T(8,128)} fusion(bf16[768,6144]{1,0:T(8,128)(2,1)} %param.18, f32[1024,768]{1,0:T(8,128)S(1)} %get-tuple-element.89, f32[768]{0:T(1024)S(1)} %copy-done.13, f32[768]{0:T(1024)S(1)} %copy-done.11, f32[1024]{0:T(1024)S(1)} %fusion.38, f32[1024]{0:T(1024)S(1)} %broadcast_multiply_fusion.2), kind=kOutput, calls=%fused_computation.95 | convolution fusion | flops 9667608576 | bytes 37763072 | tf_op jit(solution)/shard_map/dot_general | solution.py:145
  213.8 29.9 %multiply_convert_fusion.1 = (bf16[1024,3072]{1,0:T(8,128)(2,1)S(1)}, f32[1024,3072]{1,0:T(8,128)}) fusion(f32[1024,6144]{1,0:T(8,128)} %fusion.45), kind=kLoop, calls=%fused_computation.14 | loop fusion | flops 207618048 | bytes 44040192 | tf_op jit(solution)/shard_map/convert_element_type | solution.py:147
  255.1 26.7 %fusion.18 = (f32[1024,3072]{1,0:T(8,128)}, f32[1024,3072]{1,0:T(8,128)}) fusion(f32[1024,3072]{1,0:T(8,128)} %get-tuple-element.82, f32[1024,6144]{1,0:T(8,128)} %fusion.45, bf16[3072,768]{1,0:T(8,128)(2,1)} %param.19, f32[1024,768]{1,0:T(8,128)} %get-tuple-element.80, f32[1024]{0:T(1024)} %negate_multiply_fusion.2), kind=kOutput, calls=%fused_computation.42 | convolution fusion | flops 4883742720 | bytes 70782976 | tf_op jit(solution)/shard_map/dot_general | solution.py:157
  281.8 19.9 %multiply_reduce_fusion.1 = (f32[768]{0:T(1024)}, f32[1024]{0:T(1024)}, f32[768]{0:T(1024)}, f32[1024,768]{1,0:T(8,128)}) fusion(f32[1024,768]{1,0:T(8,128)} %copy-done.1, f32[1024]{0:T(1024)S(1)} %fusion.38, f32[1024]{0:T(1024)S(1)} %broadcast_multiply_fusion.2, f32[768]{0:T(1024)S(1)} %copy-done.11, bf16[768,6144]{1,0:T(8,128)(2,1)} %param.18, ...), kind=kOutput, calls=%fused_computation.50 | convolution fusion | flops 9684120576 | bytes 44065792 | tf_op jit(solution)/shard_map/dot_general | solution.py:161
  321.8 18.6 %all-to-all-done.2 = bf16[8,128,4,192]{1,0,3,2:T(8,128)(2,1)} async-done(((bf16[8,128,4,192]{1,0,3,2:T(8,128)(2,1)}), bf16[8,128,4,192]{1,0,3,2:T(8,128)(2,1)}, u32[]{:S(2)}, u32[]{:S(2)}) %all-to-all-start.2) | async-done | bytes 1572896 | tf_op jit(solution)/shard_map/all_to_all | solution.py:170
  348.2 13.7 %fusion.29 = bf16[8,3,64,512]{3,2,1,0:T(8,128)(2,1)} fusion(bf16[8,512,3,64]{1,3,2,0:T(8,128)(2,1)} %reshape.213, f32[8,3,512,512]{2,3,1,0:T(8,128)} %get-tuple-element.87, f32[8,3,512]{2,1,0:T(4,128)} %log_add_fusion), kind=kOutput, calls=%fused_computation.67 | convolution fusion | flops 818675712 | bytes 28360704 | tf_op jit(solution)/shard_map/rhqk,rqhd->rkhd/dot_general | solution.py:84
  361.9 17.3 %multiply_reduce_fusion = (f32[8,3,512]{2,1,0:T(4,128)}, f32[8,3,512,512]{2,3,1,0:T(8,128)}) fusion(f32[8,3,512,512]{2,3,1,0:T(8,128)} %get-tuple-element.87, f32[8,3,512]{2,1,0:T(4,128)} %log_add_fusion, bf16[8,512,3,64]{1,3,2,0:T(8,128)(2,1)} %reshape.213, bf16[8,512,3,3,64]{1,4,3,0,2:T(8,128)(2,1)} %reshape.209), kind=kOutput, calls=%fused_computation.1 | convolution fusion | flops 824168448 | bytes 53592064 | tf_op jit(solution)/shard_map/rqhd,rkhd->rhqk/dot_general | solution.py:70
  379.2 21.2 %multiply_convert_fusion = bf16[8,3,512,512]{2,3,1,0:T(8,128)(2,1)} fusion(f32[8,3,512,512]{2,3,1,0:T(8,128)} %get-tuple-element.94, f32[8,3,512,512]{2,3,1,0:T(8,128)} %get-tuple-element.87, f32[8,3,512]{2,1,0:T(4,128)} %get-tuple-element.93, f32[8,3,512]{2,1,0:T(4,128)} %log_add_fusion), kind=kLoop, calls=%fused_computation | loop fusion | flops 25165824 | bytes 63012864 | tf_op jit(solution)/shard_map/convert_element_type | solution.py:74
  400.4 10.1 multiply_convert_fusion.2
  410.5 8.3 multiply_convert_fusion.3
  436.1 74.3 %all_to_all.61 = bf16[8,512,3,1,192]{4,0,3,2,1:T(8,128)(2,1)} all-to-all(bf16[8,512,3,1,192]{4,0,3,2,1:T(8,128)(2,1)S(1)} %pad_maximum_fusion), channel_id=1, replica_groups=mesh['dp'=8,'head'=4] {'head'}, dimensions={1} | all-to-all | bytes 9437184 | tf_op jit(solution)/shard_map/all_to_all | solution.py:182
  510.4 8.6 copy.95
  532.5 8.0 copy.96
  546.0 10.7 fusion.42
  557.3 22.8 %fusion.25 = f32[768,6144]{1,0:T(8,128)} fusion(f32[1024,3072]{1,0:T(8,128)} %get-tuple-element.84, f32[1024,3072]{1,0:T(8,128)} %get-tuple-element.83, f32[1024,768]{1,0:T(8,128)} %copy-done.1, f32[768]{0:T(1024)S(1)} %copy-done.14, f32[768]{0:T(1024)S(1)} %copy-done.11, f32[1024]{0:T(1024)S(1)} %fusion.38, f32[1024]{0:T(1024)S(1)} %broadcast_multiply_fusion.2), kind=kOutput, calls=%fused_computation.65 | convolution fusion | flops 9680191488 | bytes 47200256 | tf_op jit(solution)/shard_map/dot_general | solution.py:160
  580.2 90.6 %reduce-scatter.13.cloned.1.call-done = f32[96,2304]{1,0:T(8,128)} async-done(((f32[768,2304]{1,0:T(8,128)}), f32[96,2304]{1,0:T(8,128)}) %reduce-scatter.13.cloned.1.call-update) | async-done | bytes 884752
  673.4 69.8 %reduce-scatter.7.cloned.1.call-done = f32[96,768]{1,0:T(8,128)} async-done(((f32[768,768]{1,0:T(8,128)}), f32[96,768]{1,0:T(8,128)}) %reduce-scatter.7.cloned.1.call-update) | async-done | bytes 294928 | tf_op jit(solution)/shard_map/reduce_scatter | solution.py:197
  743.2 166.4 %reduce-scatter.11.cloned.1.call-done = f32[384,768]{1,0:T(8,128)} async-done(((f32[3072,768]{1,0:T(8,128)}), f32[384,768]{1,0:T(8,128)}) %reduce-scatter.11.cloned.1.call-update) | async-done | bytes 1179664 | tf_op jit(solution)/shard_map/reduce_scatter | solution.py:201
  909.6 316.8 %reduce-scatter.9.cloned.1.call-done = f32[96,6144]{1,0:T(8,128)} async-done(((f32[768,6144]{1,0:T(8,128)}), f32[96,6144]{1,0:T(8,128)}) %reduce-scatter.9.cloned.1.call-update) | async-done | bytes 2359312 | tf_op jit(solution)/shard_map/reduce_scatter | solution.py:200
  1229.3 35.8 %all-reduce.6 = (f32[768]{0:T(1024)}, f32[768]{0:T(1024)}, f32[768]{0:T(1024)}, f32[768]{0:T(1024)}) all-reduce(f32[768]{0:T(1024)S(1)} %copy-done.20, f32[768]{0:T(1024)} %get-tuple-element.64, f32[768]{0:T(1024)S(1)} %copy-done.16, f32[768]{0:T(1024)S(1)} %convert_reduce_fusion), channel_id=4, replica_groups=mesh['dp'=8,'head'=4] {'dp'}, use_global_device_ids=true, to_apply=%region_16.17.clone | all-reduce | flops 3072 | bytes 24576
  1275.8 8.0 add_convert_fusion.1
  1283.8 44.4 %all-reduce.11.cloned.1.call-done = (f32[96,2304]{0,1:T(8,128)}, f32[96,768]{1,0:T(8,128)}, f32[96,6144]{1,0:T(8,128)}, f32[384,768]{1,0:T(8,128)}) async-done(((f32[96,2304]{0,1:T(8,128)}, f32[96,768]{1,0:T(8,128)}, f32[96,6144]{1,0:T(8,128)}, f32[384,768]{1,0:T(8,128)}), (f32[96,2304]{0,1:T(8,128)}, f32[96,768]{1,0:T(8,128)}, f32[96,6144]{1,0:T(8,128)}, ...) | async-done | bytes 4718608 | tf_op jit(solution)/shard_map/psum | solution.py:205
  (112 shorter events, 128.1 us)
Async XLA Ops:
  7.2 2.0 copy-start
  37.6 59.9 %all-to-all-start = ((bf16[8,128,3,4,192]{1,0,4,2,3:T(8,128)(2,1)}), bf16[8,128,3,4,192]{1,0,4,2,3:T(8,128)(2,1)}, u32[]{:S(2)}, u32[]{:S(2)}) async-start(bf16[8,128,3,4,192]{1,0,4,2,3:T(8,128)(2,1)} %copy.71), calls=%async_computation | async-start | bytes 9437184 | tf_op jit(solution)/shard_map/all_to_all | solution.py:119
  43.1 3.1 copy-start.12
  128.2 10.4 copy-start.9
  128.2 10.4 copy-start.2
  138.6 11.9 copy-start.10
  191.4 4.0 copy-start.7
  191.4 4.5 copy-start.11
  191.4 4.5 copy-start.13
  191.4 52.3 %slice-start = ((s8[4718592]{0:T(1024)(128)(4,1)}), s8[4194304]{0:T(1024)(128)(4,1)S(1)}, s32[]{:S(2)}) async-start(s8[4718592]{0:T(1024)(128)(4,1)} %bitcast.123), calls=%async_computation.13 | async-start | bytes 8388608
  195.4 48.3 %copy-start.1 = (f32[1024,768]{1,0:T(8,128)}, f32[1024,768]{1,0:T(8,128)S(1)}, u32[]{:S(2)}) copy-start(f32[1024,768]{1,0:T(8,128)S(1)} %get-tuple-element.89) | copy-start | bytes 9437188
  195.9 47.8 %slice-start.1 = ((s8[4718592]{0:T(1024)(128)(4,1)}), s8[524288]{0:T(1024)(128)(4,1)S(1)}, s32[]{:S(2)}) async-start(s8[4718592]{0:T(1024)(128)(4,1)} %bitcast.123), calls=%async_computation.14 | async-start | bytes 1048576
  243.7 5.4 copy-start.4
  243.7 5.9 copy-start.3
  243.8 5.9 copy-start.15
  249.1 2.3 copy-start.17
  302.4 5.3 copy-start.22
  306.1 1.6 copy-start.6
  306.1 234.5 %copy-start.18 = (f32[1024]{0:T(1024)}, f32[1024]{0:T(1024)S(1)}, u32[]{:S(2)}) copy-start(f32[1024]{0:T(1024)S(1)} %negate_multiply_fusion.1) | copy-start | bytes 12292
  315.9 24.5 %all-to-all-start.2 = ((bf16[8,128,4,192]{1,0,3,2:T(8,128)(2,1)}), bf16[8,128,4,192]{1,0,3,2:T(8,128)(2,1)}, u32[]{:S(2)}, u32[]{:S(2)}) async-start(bf16[8,128,4,192]{1,0,3,2:T(8,128)(2,1)} %bitcast.112), calls=%async_computation.2 | async-start | bytes 3145728 | tf_op jit(solution)/shard_map/all_to_all | solution.py:170
  320.3 350.6 %reduce-scatter.13.cloned.1.call-start = ((), (), s32[]{:S(2)}) async-start(), calls=%async_computation.11 | async-start | bytes 7962624
  519.0 7.7 copy-start.21
  524.5 2.2 copy-start.5
  540.6 202.6 %reduce-scatter.7.cloned.1.call-start = ((), (), s32[]{:S(2)}) async-start(), calls=%async_computation.8 | async-start | bytes 2654208 | tf_op jit(solution)/shard_map/reduce_scatter | solution.py:197
  545.9 363.7 %reduce-scatter.11.cloned.1.call-start = ((), (), s32[]{:S(2)}) async-start(), calls=%async_computation.10 | async-start | bytes 10616832 | tf_op jit(solution)/shard_map/reduce_scatter | solution.py:201
  556.6 669.7 %reduce-scatter.9.cloned.1.call-start = ((), (), s32[]{:S(2)}) async-start(), calls=%async_computation.9 | async-start | bytes 21233664 | tf_op jit(solution)/shard_map/reduce_scatter | solution.py:200
  580.1 646.3 %copy-start.23 = (u32[32]{0:T(128)S(1)}, u32[32]{0:T(128)}, u32[]{:S(2)}) copy-start(u32[32]{0:T(128)} %constant.103) | copy-start | bytes 388
  580.1 649.2 %copy-start.16 = (f32[768]{0:T(1024)S(1)}, f32[768]{0:T(1024)}, u32[]{:S(2)}) copy-start(f32[768]{0:T(1024)} %get-tuple-element.62) | copy-start | bytes 9220
  580.1 649.2 %copy-start.20 = (f32[768]{0:T(1024)S(1)}, f32[768]{0:T(1024)}, u32[]{:S(2)}) copy-start(f32[768]{0:T(1024)} %get-tuple-element.60) | copy-start | bytes 9220
  580.1 695.7 %copy-start.19 = (f32[1024]{0:T(1024)S(1)}, f32[1024]{0:T(1024)}, u32[]{:S(2)}) copy-start(f32[1024]{0:T(1024)} %copy-done.18) | copy-start | bytes 12292
  580.1 748.1 %all-reduce.11.cloned.1.call-start = ((), (), s32[]{:S(2)}) async-start(), calls=%async_computation.12 | async-start | bytes 10027008 | tf_op jit(solution)/shard_map/psum | solution.py:205
  1330.8 5.0 copy-start.8
  (1 other events, 0.7 us)
Sparse Core Ops, SparseCore 0:
  540.7 130.0 reduce-scatter.12
  675.3 67.8 reduce-scatter.6
  747.2 162.3 reduce-scatter.10
  913.8 312.4 reduce-scatter.8
  1229.5 98.6 all-reduce.10
where the time goes:
time: 1350 us; the launch traced here: 1340 us
  waiting for transfers between devices  756 us (56%)
  matrix products  212 us (16%)
  blocking collectives  148 us (11%)
  local copies, waits for them, and re-layouts  119 us (9%)
  other arithmetic  84.1 us (6%)
  between operations  15.1 us (1%)
    reduce_scatter x1, waiting for transfers between devices, local(): lax.psum_scatter(expand_back, 'dp', scatter_dimension=0, tiled=True)  317 us
    reduce_scatter x1, waiting for transfers between devices, local(): lax.psum_scatter(reduce_back, 'dp', scatter_dimension=0, tiled=True)  166 us
    unnamed x6, waiting for transfers between devices  90.7 us
    all_to_all x1, blocking collectives, local(): lax.all_to_all(back_joint.reshape(row_count, length, 3, 1, group_width),...  74.3 us
    reduce_scatter x1, waiting for transfers between devices, local(): lax.psum_scatter(projection_back, 'dp', scatter_dimension=0, tiled=True)  69.8 us
    all_to_all x1, waiting for transfers between devices, local(): lax.all_to_all(joint_local.reshape(row_count, quarter, 3, groups_count, g...  49.1 us
    psum x1, waiting for transfers between devices, local(): lax.psum((summed[0], summed[1], summed[2], summed[3], summed[4], summed[5...  44.4 us
    unnamed x1, blocking collectives  35.8 us
  transfers between devices with their start and end apart: 7, of which 7 were waited for; matrix products, arithmetic and copies ran while one was open for 5% of the time, Pallas kernels for 0%

commit v1 on v0

v1 whole, which is shorter than its diff:
```python
import math

import jax
import jax.numpy as jnp
import numpy as np
from jax import lax
from jax.sharding import PartitionSpec as P

H = 12
DH = 64


EPSILON = 1e-12
NEG_FILL = -1e30


def head_slopes(heads_total):
    closest = 2 ** int(math.floor(math.log2(heads_total)))

    def power_slopes(number):
        first_slope = 2.0 ** (-8.0 / number)
        return [first_slope ** (counter + 1) for counter in range(number)]

    listed = power_slopes(closest)
    listed = listed + power_slopes(2 * closest)[0::2][: heads_total - closest]
    return np.array(listed, dtype=np.float32)


def layer_norm(values, gain, offset):
    center = values - jnp.mean(values, axis=-1, keepdims=True)
    spread = jnp.mean(center * center, axis=-1, keepdims=True)
    return center * lax.rsqrt(spread + EPSILON) * gain + offset


def gated_unit(gate_up):
    half_width = gate_up.shape[-1] // 2
    return jax.nn.gelu(gate_up[:, :half_width], approximate=False) * gate_up[:, half_width:]


def masked_scores(queries, keys_block, labels, slopes):
    length = queries.shape[1]
    raw_scores = jnp.einsum(
        "rqhd,rkhd->rhqk", queries, keys_block, preferred_element_type=jnp.float32
    )
    places = jnp.arange(length)
    distance = jnp.abs(places[:, None] - places[None, :]).astype(jnp.float32)
    scores = (
        raw_scores * queries.shape[-1] ** (-0.5)
        - slopes[None, :, None, None] * distance[None, None]
    )
    matching = labels[:, None, :, None] == labels[:, None, None, :]
    return jnp.where(matching, scores, NEG_FILL)


def attend_forward(queries, keys_block, values_block, labels, slopes):
    masked = masked_scores(queries, keys_block, labels, slopes)
    row_top = jnp.max(masked, axis=-1, keepdims=True)
    exponent = jnp.exp(masked - row_top)
    row_total = jnp.sum(exponent, axis=-1, keepdims=True)
    probability = (exponent / row_total).astype(jnp.bfloat16)
    attended = jnp.einsum(
        "rhqk,rkhd->rqhd", probability, values_block, preferred_element_type=jnp.float32
    )
    return (attended, row_top + jnp.log(row_total))


def attend_backward(queries, keys_block, values_block, labels, slopes, log_total, back_out):
    masked = masked_scores(queries, keys_block, labels, slopes)
    probability = jnp.exp(masked - log_total)
    back_probs = jnp.einsum(
        "rqhd,rkhd->rhqk", back_out, values_block, preferred_element_type=jnp.float32
    )
    inner = jnp.sum(probability * back_probs, axis=-1, keepdims=True)
    back_scores = (probability * (back_probs - inner)).astype(jnp.bfloat16)
    score_scale = queries.shape[-1] ** (-0.5)
    back_queries = (
        jnp.einsum("rhqk,rkhd->rqhd", back_scores, keys_block, preferred_element_type=jnp.float32)
        * score_scale
    )
    back_keys = (
        jnp.einsum("rhqk,rqhd->rkhd", back_scores, queries, preferred_element_type=jnp.float32)
        * score_scale
    )
    back_values = jnp.einsum(
        "rhqk,rqhd->rkhd",
        probability.astype(jnp.bfloat16),
        back_out,
        preferred_element_type=jnp.float32,
    )
    return (back_queries, back_keys, back_values)


def exchange(value, axis, bit):
    sizes = (lax.axis_size("dp"), lax.axis_size("head"))
    pairs = []
    for dp in range(sizes[0]):
        for head in range(sizes[1]):
            if axis == "dp":
                target = (dp ^ (1 << bit), head)
            else:
                target = (dp, head ^ bit)
            pairs.append((dp * sizes[1] + head, target[0] * sizes[1] + target[1]))
    return lax.ppermute(value, ("dp", "head"), pairs)


def rows_to_devices(values):
    groups = lax.axis_size("head")
    me = lax.axis_index("head")
    rows, quarter, width = values.shape
    own = rows // groups
    blocks = values.reshape(groups, own, quarter, width)
    got = jnp.zeros((own, groups, quarter, width), values.dtype)
    for step in range(groups):
        block = lax.dynamic_index_in_dim(blocks, me ^ step, 0, keepdims=False)
        if step:
            block = exchange(block, "head", step)
        got = lax.dynamic_update_index_in_dim(got, block, me ^ step, 1)
    return got.reshape(own, groups * quarter, width)


def rows_from_devices(values):
    groups = lax.axis_size("head")
    me = lax.axis_index("head")
    own, length, width = values.shape
    quarter = length // groups
    blocks = values.reshape(own, groups, quarter, width)
    got = jnp.zeros((groups, own, quarter, width), values.dtype)
    for step in range(groups):
        block = lax.dynamic_index_in_dim(blocks, me ^ step, 1, keepdims=False)
        if step:
            block = exchange(block, "head", step)
        got = lax.dynamic_update_index_in_dim(got, block, me ^ step, 0)
    return got.reshape(groups * own, quarter, width)


def low(value):
    return value.astype(jnp.bfloat16)


def wide(value):
    return value.astype(jnp.float32)


def sum_over_devices(left, right_halves, order):
    dp_size = lax.axis_size("dp")
    bits = dp_size.bit_length() - 1
    dp_index = lax.axis_index("dp")
    core = lax.axis_index("head") & 1
    y_index = lax.axis_index("head") >> 1

    def product(half):
        right = lax.dynamic_index_in_dim(right_halves, half, 0, keepdims=False)
        return low(
            lax.dot_general(
                left, right, (((0,), (0,)), ((), ())), preferred_element_type=jnp.float32
            )
        )

    sent = product(1 - core)
    received = exchange(sent, "head", 1)
    kept = product(core)
    rows, columns = kept.shape
    shape = (2,) * bits + (rows // dp_size, 2, columns // 2)
    terms = [(kept.reshape(shape), {}), (received.reshape(shape), {})]
    chosen = {}

    def part(term, cut, wanted):
        starts, sizes = [], []
        for axis, size in enumerate(term.shape):
            if axis in wanted and axis not in cut:
                starts.append(wanted[axis])
                sizes.append(1)
            else:
                starts.append(0)
                sizes.append(size)
        return wide(lax.dynamic_slice(term, starts, sizes))

    def total(wanted):
        value = None
        for term, cut in terms:
            piece = part(term, cut, wanted)
            value = piece if value is None else value + piece
        return value

    y_first = "y" in order
    for step in order:
        if step == "y":
            axis, mine = bits + 1, y_index
        else:
            axis, mine = bits - 1 - step, (dp_index >> step) & 1
        away = dict(chosen)
        away[axis] = 1 - mine
        chosen[axis] = mine
        sent = low(total(away))
        got = exchange(sent, "head", 2) if step == "y" else exchange(sent, "dp", step)
        terms.append((got, dict.fromkeys(chosen)))
    own = low(total(chosen))
    if y_first:
        own = own.reshape(rows // dp_size, columns // 2)
        other = exchange(own, "head", 2)
        own = jnp.where(
            y_index == 0,
            jnp.concatenate((own, other), axis=-1),
            jnp.concatenate((other, own), axis=-1),
        )
    else:
        own = own.reshape(rows // dp_size, columns)
        own = low(wide(own) + wide(exchange(own, "head", 2)))
    other = exchange(own, "head", 1)
    return jnp.where(core == 0, jnp.stack((own, other)), jnp.stack((other, own)))


def halves(value):
    width = value.shape[1] // 2
    return jnp.stack((value[:, :width], value[:, width:]))


def join_halves(value):
    return wide(jnp.concatenate((value[0], value[1]), axis=-1))


def local(
    tokens,
    segment_labels,
    joint_projection,
    output_projection,
    first_gain,
    first_offset,
    expand_weight,
    reduce_weight,
    second_gain,
    second_offset,
    cotangent,
):
    model_width = tokens.shape[2]
    length = segment_labels.shape[1]
    groups_count = lax.axis_size("head")
    group_index = lax.axis_index("head")
    bits = lax.axis_size("dp").bit_length() - 1
    up_order = tuple(range(bits))
    down_order = tuple(range(1, bits)) + (0,)
    inner = expand_weight.shape[1] // 2
    slopes = jnp.asarray(head_slopes(H), dtype=jnp.float32)
    own_tokens = rows_to_devices(tokens)
    own_cotangent = rows_to_devices(cotangent)
    row_count = own_tokens.shape[0]
    labels = lax.dynamic_slice_in_dim(segment_labels, group_index * row_count, row_count)
    flat_tokens = own_tokens.reshape(-1, model_width)
    joint = low(jnp.dot(flat_tokens, joint_projection, preferred_element_type=jnp.float32))
    joint_heads = joint.reshape(row_count, length, 3, H, DH)
    queries = joint_heads[:, :, 0]
    keys_block = joint_heads[:, :, 1]
    values_block = joint_heads[:, :, 2]
    attended, log_total = attend_forward(queries, keys_block, values_block, labels, slopes)
    token_heads = low(attended).reshape(-1, model_width)
    branch = jnp.dot(token_heads, output_projection, preferred_element_type=jnp.float32)
    hidden, first_norm_back = jax.vjp(
        layer_norm, wide(flat_tokens) + branch, first_gain, first_offset
    )
    hidden_low = low(hidden)
    gate_up = jnp.dot(hidden_low, expand_weight, preferred_element_type=jnp.float32)
    active, gated_back = jax.vjp(gated_unit, gate_up)
    active_low = low(active)
    mixed = jnp.dot(active_low, reduce_weight, preferred_element_type=jnp.float32)
    output, second_norm_back = jax.vjp(layer_norm, hidden + mixed, second_gain, second_offset)
    layer_output = rows_from_devices(low(output).reshape(own_tokens.shape))
    back_two, second_gain_back, second_offset_back = second_norm_back(
        wide(own_cotangent.reshape(-1, model_width))
    )
    back_mixed = low(back_two)
    reduce_sum = sum_over_devices(active_low, halves(back_mixed), up_order)
    (back_gate_up,) = gated_back(
        jnp.dot(back_mixed, reduce_weight.T, preferred_element_type=jnp.float32)
    )
    back_gate_up = low(back_gate_up)
    expand_sums = []
    for number, order in enumerate((down_order, ("y",) + up_order)):
        start = number * (inner // 2)
        part = jnp.stack(
            (
                back_gate_up[:, start : start + inner // 2],
                back_gate_up[:, inner + start : inner + start + inner // 2],
            )
        )
        expand_sums.append(sum_over_devices(hidden_low, part, order))
    back_hidden = back_two + jnp.dot(
        back_gate_up, expand_weight.T, preferred_element_type=jnp.float32
    )
    back_one, first_gain_back, first_offset_back = first_norm_back(back_hidden)
    back_branch = low(back_one)
    projection_sum = sum_over_devices(token_heads, halves(back_branch), up_order)
    back_attended = low(
        jnp.dot(back_branch, output_projection.T, preferred_element_type=jnp.float32)
    ).reshape(row_count, length, H, DH)
    back_queries, back_keys, back_values = attend_backward(
        queries, keys_block, values_block, labels, slopes, log_total, back_attended
    )
    back_joint = low(jnp.stack((back_queries, back_keys, back_values), axis=2)).reshape(
        -1, 3 * model_width
    )
    joint_sum = sum_over_devices(flat_tokens, halves(back_joint), down_order)
    tokens_back = back_one + jnp.dot(
        back_joint, joint_projection.T, preferred_element_type=jnp.float32
    )
    tokens_gradient = rows_from_devices(low(tokens_back).reshape(own_tokens.shape))
    vectors = lax.psum(
        jnp.stack((first_gain_back, first_offset_back, second_gain_back, second_offset_back)),
        ("dp", "head"),
    )
    own_width = model_width // lax.axis_size("dp")
    vectors = lax.dynamic_slice_in_dim(
        vectors, lax.axis_index("dp") * own_width, own_width, axis=1
    )
    expand_gradient = wide(
        jnp.concatenate(
            (expand_sums[0][0], expand_sums[1][0], expand_sums[0][1], expand_sums[1][1]), axis=-1
        )
    )
    return (
        layer_output,
        tokens_gradient,
        join_halves(joint_sum),
        join_halves(projection_sum),
        vectors[0],
        vectors[1],
        expand_gradient,
        join_halves(reduce_sum),
        vectors[2],
        vectors[3],
    )


def solution(mesh):
    placed = (
        P("dp", "head", None),
        P("dp", None),
        P(),
        P(),
        P(),
        P(),
        P(),
        P(),
        P(),
        P(),
        P("dp", "head", None),
    )
    return jax.shard_map(
        local,
        mesh=mesh,
        in_specs=placed,
        out_specs=(
            P("dp", "head", None),
            P("dp", "head", None),
            P("dp", None),
            P("dp", None),
            P("dp"),
            P("dp"),
            P("dp", None),
            P("dp", None),
            P("dp"),
            P("dp"),
        ),
        check_vma=False,
    )
```

time: 1350 us -> 732 us (0.54)
  waiting for transfers between devices: 756 us -> 71.5 us
  blocking collectives: 148 us -> 41 us
  local copies, waits for them, and re-layouts: 119 us -> 224 us
  other arithmetic: 84.1 us -> 147 us
  starting transfers between devices: 10 us -> 36.6 us
    reduce_scatter x3 -> x0, waiting for transfers between devices: 553 us -> none  [the longest x1 317 us: local(): lax.psum_scatter(expand_back, 'dp', scatter_dimension=0, tiled=True)]
    all_to_all x2 -> x0, blocking collectives: 105 us -> none  [the longest x1 74.3 us: local(): lax.all_to_all(back_joint.reshape(row_count, length, 3, 1, group_width),...]
    unnamed x6 -> x0, waiting for transfers between devices: 90.7 us -> none
    ppermute x0 -> x43, waiting for transfers between devices: none -> 71.5 us  [exchange(): return lax.ppermute(value, ('dp', 'head'), pairs)]
    all_to_all x2 -> x0, waiting for transfers between devices: 67.7 us -> none  [the longest x1 49.1 us: local(): lax.all_to_all(joint_local.reshape(row_count, quarter, 3, groups_count, g...]
    convert_element_type x1 -> x34, other arithmetic: 29.9 us -> 86.5 us  [the longest x30 82.1 us: low(): return value.astype(jnp.bfloat16)]
    psum x1 -> x0, waiting for transfers between devices: 44.4 us -> none  [local(): lax.psum((summed[0], summed[1], summed[2], summed[3], summed[4], summed[5...]
    reshape x4 -> x18, local copies, waits for them, and re-layouts: 33.2 us -> 73.7 us  [the longest x10 57.6 us: sum_over_devices(): terms = [(kept.reshape(shape), {}), (received.reshape(shape), {})]]
  transfers between devices with their start and end apart: 7 -> 43, of which waited for: 7 -> 12; matrix products, arithmetic and copies ran while one was open for 5% -> 47% of each run, Pallas kernels for 0% -> 0%
where the time goes in v1:
time: 732 us; the launch traced here: 725 us
  local copies, waits for them, and re-layouts  224 us (31%)
  matrix products  204 us (28%)
  other arithmetic  147 us (20%)
  waiting for transfers between devices  71.5 us (10%)
  blocking collectives  41 us (6%)
  starting transfers between devices  36.6 us (5%)
    convert_element_type x30, other arithmetic, low(): return value.astype(jnp.bfloat16)  82.1 us
    ppermute x43, waiting for transfers between devices, exchange(): return lax.ppermute(value, ('dp', 'head'), pairs)  71.5 us
    reshape x10, local copies, waits for them, and re-layouts, sum_over_devices(): terms = [(kept.reshape(shape), {}), (received.reshape(shape), {})]  57.6 us
    unnamed x130, local copies, waits for them, and re-layouts  44.3 us
    dot_general x10, matrix products, product(): lax.dot_general(left, right, (((0,), (0,)), ((), ())), preferred_element_...  41.5 us
    psum x1, blocking collectives, local(): lax.psum(jnp.stack((first_gain_back, first_offset_back, second_gain_back,...  41 us
    ppermute x43, starting transfers between devices, exchange(): return lax.ppermute(value, ('dp', 'head'), pairs)  36.6 us
    dynamic_slice x13, local copies, waits for them, and re-layouts, part(): return wide(lax.dynamic_slice(term, starts, sizes))  34.7 us
  transfers between devices with their start and end apart: 43, of which 12 were waited for; matrix products, arithmetic and copies ran while one was open for 47% of the time, Pallas kernels for 0%

profile of v1, /device:TPU:0, one launch (start us, length us, event | category | flops | bytes accessed | tf_op | source)
XLA Modules:
  0.0 725.5 jit_solution(14826927459982976827)
XLA Ops:
  11.2 7.6 %broadcast_multiply_fusion = f32[12,512,512]{1,2,0:T(8,128)} fusion(f32[512,512]{0,1:T(8,128)} %abs_convert_fusion, f32[12]{0:T(128)S(1)} %copy-done.53), kind=kLoop, calls=%fused_computation.39 | loop fusion | flops 3145728 | bytes 13631536 | tf_op jit(solution)/shard_map/mul | solution.py:49
  31.3 7.9 %convolution_convert_fusion = bf16[1024,2304]{1,0:T(8,128)(2,1)} fusion(bf16[1024,768]{1,0:T(8,128)(2,1)} %bitcast.8, bf16[768,2304]{1,0:T(8,128)(2,1)S(1)} %copy-done), kind=kOutput, calls=%fused_computation.40 | convolution fusion | flops 3626237952 | bytes 9830400 | tf_op jit(solution)/shard_map/dot_general | solution.py:249
  39.2 6.7 copy.102
  45.9 8.8 %reshape.265 = bf16[2,512,3,12,64]{1,0,4,3,2:T(2,128)(2,1)} reshape(bf16[1024,2304]{0,1:T(8,128)(2,1)} %copy.102) | data formatting | bytes 9437184 | tf_op jit(solution)/shard_map/reshape | solution.py:250
  54.7 6.4 fusion.89
  61.2 17.5 %fusion.90 = (f32[2,12,512]{2,1,0:T(8,128)}, f32[2,12,512,512]{2,3,1,0:T(8,128)}) fusion(f32[12,512,512]{1,2,0:T(8,128)} %broadcast_multiply_fusion, bf16[2,512,1,12,64]{1,0,4,3,2:T(2,128)(2,1)} %get-tuple-element.63, bf16[2,512,1,12,64]{1,0,4,3,2:T(2,128)(2,1)} %get-tuple-element.62, pred[2,512,512]{1,2,0:T(8,128)(4,1)} %broadcast_compare_fusion), kind=kOutput, calls=%fused_computation.268 | convolution fusion | flops 830459904 | bytes 41467904 | tf_op jit(solution)/shard_map/rqhd,rkhd->rhqk/dot_general | solution.py:42
  78.7 10.3 %fusion = f32[2,12,512]{2,1,0:T(8,128)S(1)} fusion(f32[2,12,512,512]{2,3,1,0:T(8,128)} %get-tuple-element.104, f32[2,12,512]{2,1,0:T(8,128)} %get-tuple-element.103), kind=kLoop, calls=%fused_computation.7 | loop fusion | flops 12570624 | bytes 25264128 | tf_op jit(solution)/shard_map/reduce_sum | solution.py:59
  89.0 10.9 %fusion.47 = bf16[2,512,12,64]{1,3,2,0:T(8,128)(2,1)S(1)} fusion(f32[2,12,512,512]{2,3,1,0:T(8,128)} %get-tuple-element.104, f32[2,12,512]{2,1,0:T(8,128)S(1)} %fusion, f32[2,12,512]{2,1,0:T(8,128)S(1)} %copy-done.37, bf16[2,512,1,12,64]{1,0,4,3,2:T(2,128)(2,1)S(1)} %copy-done.14), kind=kOutput, calls=%fused_computation.118 | convolution fusion | flops 824967168 | bytes 28409856 | tf_op jit(solution)/shard_map/rhqk,rkhd->rqhd/dot_general | solution.py:61
  108.7 13.3 %fusion.92 = f32[1024,6144]{1,0:T(8,128)} fusion(bf16[1024,768]{1,0:T(8,128)(2,1)S(1)} %fusion.31, bf16[768,6144]{1,0:T(8,128)(2,1)S(1)} %bitcast.280), kind=kOutput, calls=%fused_computation.270 | convolution fusion | flops 9663676416 | bytes 36175872 | tf_op jit(solution)/shard_map/dot_general | solution.py:261
  122.0 29.9 %multiply_convert_fusion.1 = (bf16[1024,3072]{1,0:T(8,128)(2,1)S(1)}, f32[1024,3072]{1,0:T(8,128)}) fusion(f32[1024,6144]{1,0:T(8,128)} %fusion.92), kind=kLoop, calls=%fused_computation.14 | loop fusion | flops 207618048 | bytes 44040192 | tf_op jit(solution)/shard_map/convert_element_type | solution.py:137
  151.9 7.7 %fusion.91 = (f32[1024]{0:T(1024)S(1)}, f32[1024,768]{1,0:T(8,128)S(1)}) fusion(bf16[1024,3072]{1,0:T(8,128)(2,1)S(1)} %get-tuple-element.49, bf16[3072,768]{1,0:T(8,128)(2,1)} %param.19, f32[768]{0:T(1024)S(1)} %copy-done.49, f32[768]{0:T(1024)S(1)} %copy-done.44, f32[1024]{0:T(1024)S(1)} %fusion.73, f32[1024,768]{1,0:T(8,128)S(1)} %get-tuple-element.52, ...), kind=kOutput, calls=%fused_computation.269 | convolution fusion | flops 4836555776 | bytes 17319936 | tf_op jit(solution)/shard_map/dot_general | solution.py:264
  183.9 26.4 %fusion.13 = (f32[1024,3072]{1,0:T(8,128)}, f32[1024,3072]{1,0:T(8,128)}) fusion(f32[1024,3072]{1,0:T(8,128)} %get-tuple-element.50, f32[1024,6144]{1,0:T(8,128)} %fusion.92, bf16[1024,768]{1,0:T(8,128)(2,1)S(1)} %add_convert_fusion.4, bf16[3072,768]{1,0:T(8,128)(2,1)} %param.19), kind=kOutput, calls=%fused_computation.50 | convolution fusion | flops 4882169856 | bytes 69206016 | tf_op jit(solution)/shard_map/dot_general | solution.py:273
  210.3 9.3 %add_convert_fusion = bf16[1024,6144]{1,0:T(8,128)(2,1)S(1)} fusion(f32[1024,3072]{1,0:T(8,128)} %get-tuple-element.54, f32[1024,3072]{1,0:T(8,128)} %get-tuple-element.53), kind=kLoop, calls=%fused_computation.3 | loop fusion | flops 12582912 | bytes 37748736 | tf_op jit(solution)/shard_map/convert_element_type | solution.py:137
  242.2 19.5 %multiply_reduce_fusion.1 = (f32[768]{0:T(1024)}, f32[1024]{0:T(1024)}, f32[768]{0:T(1024)}, f32[1024,768]{1,0:T(8,128)}) fusion(f32[1024,768]{1,0:T(8,128)} %copy-done.3, f32[1024]{0:T(1024)S(1)} %fusion.73, f32[1024]{0:T(1024)S(1)} %broadcast_multiply_fusion.2, f32[768]{0:T(1024)S(1)} %copy-done.44, bf16[1024,6144]{1,0:T(8,128)(2,1)} %copy-done.2, ...), kind=kOutput, calls=%fused_computation.76 | convolution fusion | flops 9671537664 | bytes 31482880 | tf_op jit(solution)/shard_map/dot_general | solution.py:286
  284.2 20.6 %multiply_reduce_fusion = (f32[2,12,512]{2,1,0:T(8,128)}, f32[2,12,512,512]{2,3,1,0:T(8,128)}) fusion(f32[2,12,512,512]{2,3,1,0:T(8,128)} %get-tuple-element.104, f32[2,12,512]{2,1,0:T(8,128)} %log_add_fusion, bf16[2,512,1,12,64]{1,0,4,3,2:T(2,128)(2,1)} %get-tuple-element.61, bf16[2,512,12,64]{1,0,3,2:T(2,128)(2,1)} %reshape.269), kind=kOutput, calls=%fused_computation.1 | convolution fusion | flops 824168448 | bytes 53575680 | tf_op jit(solution)/shard_map/rqhd,rkhd->rhqk/dot_general | solution.py:70
  304.8 17.6 %multiply_convert_fusion = bf16[2,12,512,512]{2,3,1,0:T(8,128)(2,1)S(1)} fusion(f32[2,12,512,512]{2,3,1,0:T(8,128)} %get-tuple-element.109, f32[2,12,512,512]{2,3,1,0:T(8,128)} %get-tuple-element.104, f32[2,12,512]{2,1,0:T(8,128)} %get-tuple-element.108, f32[2,12,512]{2,1,0:T(8,128)} %log_add_fusion), kind=kLoop, calls=%fused_computation | loop fusion | flops 25165824 | bytes 63012864 | tf_op jit(solution)/shard_map/convert_element_type | solution.py:74
  330.3 9.7 %fusion.46 = bf16[2,512,1,12,64]{1,4,3,0,2:T(8,128)(2,1)} fusion(bf16[2,12,512,512]{2,3,1,0:T(8,128)(2,1)} %copy-done.1, bf16[2,512,1,12,64]{1,0,4,3,2:T(2,128)(2,1)S(1)} %copy-done.7), kind=kOutput, calls=%fused_computation.117 | convolution fusion | flops 806879232 | bytes 15728640 | tf_op jit(solution)/shard_map/rhqk,rqhd->rkhd/dot_general | solution.py:81
  340.0 13.7 %fusion.42 = bf16[2,512,1,12,64]{1,4,3,0,2:T(8,128)(2,1)} fusion(f32[2,12,512,512]{2,3,1,0:T(8,128)} %get-tuple-element.104, f32[2,12,512]{2,1,0:T(8,128)} %log_add_fusion, bf16[2,512,12,64]{1,0,3,2:T(2,128)(2,1)} %reshape.269), kind=kOutput, calls=%fused_computation.115 | convolution fusion | flops 818675712 | bytes 28360704 | tf_op jit(solution)/shard_map/rhqk,rqhd->rkhd/dot_general | solution.py:84
  358.8 9.6 %copy.114 = bf16[2,512,3,12,64]{1,0,4,3,2:T(2,128)(2,1)} copy(bf16[2,512,3,12,64]{1,4,3,0,2:T(8,128)(2,1)} %pad_maximum_fusion) | data formatting | bytes 9437184 | tf_op jit(solution)/shard_map/stack | solution.py:298
  380.5 7.9 %reshape.291 = bf16[2,2,2,384,2,192]{5,4,3,2,1,0:T(2,128)(2,1)} reshape(bf16[3072,384]{1,0:T(8,128)(2,1)} %convolution_convert_fusion.2) | data formatting | bytes 4718592 | tf_op jit(solution)/shard_map/reshape | solution.py:164
  388.9 6.0 reshape.284
  394.9 5.8 constant_dynamic-slice_fusion.3
  407.1 41.0 %psum.7 = f32[4,768]{1,0:T(4,128)} all-reduce(f32[4,768]{1,0:T(4,128)S(1)} %pad_maximum_fusion.1), channel_id=1, replica_groups=mesh['dp'=8,'head'=4] {'dp','head'}, use_global_device_ids=true, to_apply=%region_15.16 | all-reduce | flops 3072 | bytes 24576 | tf_op jit(solution)/shard_map/psum | solution.py:306
  492.4 6.4 reshape.281
  537.0 8.6 %collective-permute-done.5 = bf16[2,128,768]{2,1,0:T(8,128)(2,1)S(1)} collective-permute-done((bf16[2,128,768]{2,1,0:T(8,128)(2,1)}, bf16[2,128,768]{2,1,0:T(8,128)(2,1)S(1)}, u32[]{:S(2)}, u32[]{:S(2)}) %collective-permute-start.5) | collective-permute-done | bytes 393248 | tf_op jit(solution)/shard_map/ppermute | solution.py:103
  556.7 7.9 %reshape.292 = bf16[2,2,2,384,2,192]{5,4,3,2,1,0:T(2,128)(2,1)} reshape(bf16[3072,384]{1,0:T(8,128)(2,1)} %collective-permute-done.37) | data formatting | bytes 4718592 | tf_op jit(solution)/shard_map/reshape | solution.py:164
  577.2 6.1 reshape.282
  589.2 6.0 reshape.285
  611.6 13.3 %collective-permute-done.14 = bf16[1,1,2,96,2,576]{5,4,3,2,1,0:T(2,128)(2,1)S(1)} collective-permute-done((bf16[1,1,2,96,2,576]{5,4,3,2,1,0:T(2,128)(2,1)S(1)}, bf16[1,1,2,96,2,576]{5,4,3,2,1,0:T(2,128)(2,1)S(1)}, u32[]{:S(2)}, u32[]{:S(2)}) %collective-permute-start.14) | collective-permute-done | bytes 442400 | tf_op jit(solution)/shard_map/ppermute | solution.py:103
  659.1 13.6 %collective-permute-done.32 = bf16[2,2,1,96,1,768]{5,3,4,2,1,0:T(8,128)(2,1)S(1)} collective-permute-done((bf16[2,2,1,96,1,768]{5,3,4,2,1,0:T(8,128)(2,1)S(1)}, bf16[2,2,1,96,1,768]{5,3,4,2,1,0:T(8,128)(2,1)S(1)}, u32[]{:S(2)}, u32[]{:S(2)}) %collective-permute-start.32) | collective-permute-done | bytes 589856 | tf_op jit(solution)/shard_map/ppermute | solution.py:103
  677.9 6.3 collective-permute-done.26
  690.4 9.0 %collective-permute-done.40 = bf16[1,1,1,384,2,192]{3,5,4,2,1,0:T(8,128)(2,1)S(1)} collective-permute-done((bf16[1,1,1,384,2,192]{3,5,4,2,1,0:T(8,128)(2,1)S(1)}, bf16[1,1,1,384,2,192]{3,5,4,2,1,0:T(8,128)(2,1)S(1)}, u32[]{:S(2)}, u32[]{:S(2)}) %collective-permute-start.40) | collective-permute-done | bytes 294944 | tf_op jit(solution)/shard_map/ppermute | solution.py:103
  (344 shorter events, 332.5 us)
Async XLA Ops:
  3.1 22.9 %collective-permute-start = (bf16[2,128,768]{2,1,0:T(8,128)(2,1)}, bf16[2,128,768]{2,1,0:T(8,128)(2,1)}, u32[]{:S(2)}, u32[]{:S(2)}) collective-permute-start(bf16[2,128,768]{2,1,0:T(8,128)(2,1)} %get-tuple-element.88), channel_id=1, source_target_pairs={{0,1},{1,0},{2,3},{3,2},{4,5},{5,4},{6,7},{7,6},{8,9},{9,8},{10,11... | collective-permute-start | bytes 1179656 | tf_op jit(solution)/shard_map/ppermute | solution.py:103
  3.6 24.2 %collective-permute-start.1 = (bf16[2,128,768]{2,1,0:T(8,128)(2,1)}, bf16[2,128,768]{2,1,0:T(8,128)(2,1)}, u32[]{:S(2)}, u32[]{:S(2)}) collective-permute-start(bf16[2,128,768]{2,1,0:T(8,128)(2,1)} %get-tuple-element.87), channel_id=1, source_target_pairs={{0,2},{1,3},{2,0},{3,1},{4,6},{5,7},{6,4},{7,5},{8,10},{9,11},{10,... | collective-permute-start | bytes 1179656 | tf_op jit(solution)/shard_map/ppermute | solution.py:103
  6.1 23.4 %collective-permute-start.2 = (bf16[2,128,768]{2,1,0:T(8,128)(2,1)}, bf16[2,128,768]{2,1,0:T(8,128)(2,1)}, u32[]{:S(2)}, u32[]{:S(2)}) collective-permute-start(bf16[2,128,768]{2,1,0:T(8,128)(2,1)} %get-tuple-element.86), channel_id=1, source_target_pairs={{0,3},{1,2},{2,1},{3,0},{4,7},{5,6},{6,5},{7,4},{8,11},{9,10},{10,... | collective-permute-start | bytes 1179656 | tf_op jit(solution)/shard_map/ppermute | solution.py:103
  7.3 152.8 %collective-permute-start.6 = (bf16[2,128,768]{2,1,0:T(8,128)(2,1)}, bf16[2,128,768]{2,1,0:T(8,128)(2,1)}, u32[]{:S(2)}, u32[]{:S(2)}) collective-permute-start(bf16[2,128,768]{2,1,0:T(8,128)(2,1)} %get-tuple-element.82), channel_id=1, source_target_pairs={{0,1},{1,0},{2,3},{3,2},{4,5},{5,4},{6,7},{7,6},{8,9},{9,8},{10,11... | collective-permute-start | bytes 1179656 | tf_op jit(solution)/shard_map/ppermute | solution.py:103
  7.4 154.5 %collective-permute-start.7 = (bf16[2,128,768]{2,1,0:T(8,128)(2,1)}, bf16[2,128,768]{2,1,0:T(8,128)(2,1)}, u32[]{:S(2)}, u32[]{:S(2)}) collective-permute-start(bf16[2,128,768]{2,1,0:T(8,128)(2,1)} %get-tuple-element.81), channel_id=1, source_target_pairs={{0,2},{1,3},{2,0},{3,1},{4,6},{5,7},{6,4},{7,5},{8,10},{9,11},{10,... | collective-permute-start | bytes 1179656 | tf_op jit(solution)/shard_map/ppermute | solution.py:103
  26.0 137.8 %collective-permute-start.8 = (bf16[2,128,768]{2,1,0:T(8,128)(2,1)}, bf16[2,128,768]{2,1,0:T(8,128)(2,1)}, u32[]{:S(2)}, u32[]{:S(2)}) collective-permute-start(bf16[2,128,768]{2,1,0:T(8,128)(2,1)} %get-tuple-element.80), channel_id=1, source_target_pairs={{0,3},{1,2},{2,1},{3,0},{4,7},{5,6},{6,5},{7,4},{8,11},{9,10},{10,... | collective-permute-start | bytes 1179656 | tf_op jit(solution)/shard_map/ppermute | solution.py:103
  388.4 168.3 %collective-permute-start.37 = (bf16[3072,384]{1,0:T(8,128)(2,1)}, bf16[3072,384]{1,0:T(8,128)(2,1)}, u32[]{:S(2)}, u32[]{:S(2)}) collective-permute-start(bf16[3072,384]{1,0:T(8,128)(2,1)} %convolution_convert_fusion.1), channel_id=1, source_target_pairs={{0,1},{1,0},{2,3},{3,2},{4,5},{5,4},{6,7},{7,6},{8,9},{9,8},{10,11... | collective-permute-start | bytes 7077896 | tf_op jit(solution)/shard_map/ppermute | solution.py:103
  388.6 188.5 %collective-permute-start.24 = (bf16[768,1536]{1,0:T(8,128)(2,1)}, bf16[768,1536]{1,0:T(8,128)(2,1)}, u32[]{:S(2)}, u32[]{:S(2)}) collective-permute-start(bf16[768,1536]{1,0:T(8,128)(2,1)} %convolution_convert_fusion.5), channel_id=1, source_target_pairs={{0,1},{1,0},{2,3},{3,2},{4,5},{5,4},{6,7},{7,6},{8,9},{9,8},{10,11... | collective-permute-start | bytes 7077896 | tf_op jit(solution)/shard_map/ppermute | solution.py:103
  452.6 22.9 %collective-permute-start.18 = (bf16[768,384]{1,0:T(8,128)(2,1)}, bf16[768,384]{1,0:T(8,128)(2,1)}, u32[]{:S(2)}, u32[]{:S(2)}) collective-permute-start(bf16[768,384]{1,0:T(8,128)(2,1)} %convolution_convert_fusion.10), channel_id=1, source_target_pairs={{0,1},{1,0},{2,3},{3,2},{4,5},{5,4},{6,7},{7,6},{8,9},{9,8},{10,11... | collective-permute-start | bytes 1769480 | tf_op jit(solution)/shard_map/ppermute | solution.py:103
  455.1 49.1 %collective-permute-start.9 = (bf16[2,128,768]{2,1,0:T(8,128)(2,1)}, bf16[2,128,768]{2,1,0:T(8,128)(2,1)}, u32[]{:S(2)}, u32[]{:S(2)}) collective-permute-start(bf16[2,128,768]{2,1,0:T(8,128)(2,1)} %get-tuple-element.79), channel_id=1, source_target_pairs={{0,1},{1,0},{2,3},{3,2},{4,5},{5,4},{6,7},{7,6},{8,9},{9,8},{10,11... | collective-permute-start | bytes 1179656 | tf_op jit(solution)/shard_map/ppermute | solution.py:103
  456.7 51.8 %collective-permute-start.10 = (bf16[2,128,768]{2,1,0:T(8,128)(2,1)}, bf16[2,128,768]{2,1,0:T(8,128)(2,1)}, u32[]{:S(2)}, u32[]{:S(2)}) collective-permute-start(bf16[2,128,768]{2,1,0:T(8,128)(2,1)} %get-tuple-element.78), channel_id=1, source_target_pairs={{0,2},{1,3},{2,0},{3,1},{4,6},{5,7},{6,4},{7,5},{8,10},{9,11},{10,... | collective-permute-start | bytes 1179656 | tf_op jit(solution)/shard_map/ppermute | solution.py:103
  481.0 25.0 %collective-permute-start.19 = (bf16[2,2,1,96,2,192]{5,4,3,2,1,0:T(2,128)(2,1)}, bf16[2,2,1,96,2,192]{5,4,3,2,1,0:T(2,128)(2,1)}, u32[]{:S(2)}, u32[]{:S(2)}) collective-permute-start(bf16[2,2,1,96,2,192]{5,4,3,2,1,0:T(2,128)(2,1)} %add_convert_fusion.13), channel_id=1, source_target_pairs={{0,4},{1,5},{2,6},{3,7},{4,0},{5,1},{6,2},{7,3},{8,12},{9,13},{10,... | collective-permute-start | bytes 884744 | tf_op jit(solution)/shard_map/ppermute | solution.py:103
  504.2 12.4 %collective-permute-start.11 = (bf16[2,128,768]{2,1,0:T(8,128)(2,1)}, bf16[2,128,768]{2,1,0:T(8,128)(2,1)S(1)}, u32[]{:S(2)}, u32[]{:S(2)}) collective-permute-start(bf16[2,128,768]{2,1,0:T(8,128)(2,1)} %get-tuple-element.77), channel_id=1, source_target_pairs={{0,3},{1,2},{2,1},{3,0},{4,7},{5,6},{6,5},{7,4},{8,11},{9,10},{10,... | collective-permute-start | bytes 1179656 | tf_op jit(solution)/shard_map/ppermute | solution.py:103
  506.0 11.7 %collective-permute-start.3 = (bf16[2,128,768]{2,1,0:T(8,128)(2,1)}, bf16[2,128,768]{2,1,0:T(8,128)(2,1)}, u32[]{:S(2)}, u32[]{:S(2)}) collective-permute-start(bf16[2,128,768]{2,1,0:T(8,128)(2,1)} %get-tuple-element.85), channel_id=1, source_target_pairs={{0,1},{1,0},{2,3},{3,2},{4,5},{5,4},{6,7},{7,6},{8,9},{9,8},{10,11... | collective-permute-start | bytes 1179656 | tf_op jit(solution)/shard_map/ppermute | solution.py:103
  515.4 32.3 %collective-permute-start.12 = (bf16[768,1152]{1,0:T(8,128)(2,1)}, bf16[768,1152]{1,0:T(8,128)(2,1)}, u32[]{:S(2)}, u32[]{:S(2)}) collective-permute-start(bf16[768,1152]{1,0:T(8,128)(2,1)} %convolution_convert_fusion.7), channel_id=1, source_target_pairs={{0,1},{1,0},{2,3},{3,2},{4,5},{5,4},{6,7},{7,6},{8,9},{9,8},{10,11... | collective-permute-start | bytes 5308424 | tf_op jit(solution)/shard_map/ppermute | solution.py:103
  516.6 12.6 %collective-permute-start.4 = (bf16[2,128,768]{2,1,0:T(8,128)(2,1)}, bf16[2,128,768]{2,1,0:T(8,128)(2,1)}, u32[]{:S(2)}, u32[]{:S(2)}) collective-permute-start(bf16[2,128,768]{2,1,0:T(8,128)(2,1)} %get-tuple-element.84), channel_id=1, source_target_pairs={{0,2},{1,3},{2,0},{3,1},{4,6},{5,7},{6,4},{7,5},{8,10},{9,11},{10,... | collective-permute-start | bytes 1179656 | tf_op jit(solution)/shard_map/ppermute | solution.py:103
  525.6 63.6 %collective-permute-start.30 = (bf16[768,1536]{1,0:T(8,128)(2,1)}, bf16[768,1536]{1,0:T(8,128)(2,1)}, u32[]{:S(2)}, u32[]{:S(2)}) collective-permute-start(bf16[768,1536]{1,0:T(8,128)(2,1)} %convolution_convert_fusion.3), channel_id=1, source_target_pairs={{0,1},{1,0},{2,3},{3,2},{4,5},{5,4},{6,7},{7,6},{8,9},{9,8},{10,11... | collective-permute-start | bytes 7077896 | tf_op jit(solution)/shard_map/ppermute | solution.py:103
  534.1 11.5 %collective-permute-start.5 = (bf16[2,128,768]{2,1,0:T(8,128)(2,1)}, bf16[2,128,768]{2,1,0:T(8,128)(2,1)S(1)}, u32[]{:S(2)}, u32[]{:S(2)}) collective-permute-start(bf16[2,128,768]{2,1,0:T(8,128)(2,1)} %get-tuple-element.83), channel_id=1, source_target_pairs={{0,3},{1,2},{2,1},{3,0},{4,7},{5,6},{6,5},{7,4},{8,11},{9,10},{10,... | collective-permute-start | bytes 1179656 | tf_op jit(solution)/shard_map/ppermute | solution.py:103
  556.5 43.1 %collective-permute-start.13 = (bf16[2,1,2,96,2,576]{5,4,3,2,1,0:T(2,128)(2,1)}, bf16[2,1,2,96,2,576]{5,4,3,2,1,0:T(2,128)(2,1)}, u32[]{:S(2)}, u32[]{:S(2)}) collective-permute-start(bf16[2,1,2,96,2,576]{5,4,3,2,1,0:T(2,128)(2,1)} %add_convert_fusion.8), channel_id=1, source_target_pairs={{0,8},{1,9},{2,10},{3,11},{4,12},{5,13},{6,14},{7,15},{8,0},{9,1},... | collective-permute-start | bytes 2654216 | tf_op jit(solution)/shard_map/ppermute | solution.py:103
  575.9 71.9 %collective-permute-start.38 = (bf16[2,2,1,384,2,192]{3,5,4,2,1,0:T(8,128)(2,1)}, bf16[2,2,1,384,2,192]{3,5,4,2,1,0:T(8,128)(2,1)}, u32[]{:S(2)}, u32[]{:S(2)}) collective-permute-start(bf16[2,2,1,384,2,192]{3,5,4,2,1,0:T(8,128)(2,1)} %add_convert_fusion.5), channel_id=1, source_target_pairs={{0,4},{1,5},{2,6},{3,7},{4,0},{5,1},{6,2},{7,3},{8,12},{9,13},{10,... | collective-permute-start | bytes 3538952 | tf_op jit(solution)/shard_map/ppermute | solution.py:103
  587.2 65.6 %collective-permute-start.25 = (bf16[2,1,2,96,2,768]{5,4,3,2,1,0:T(2,128)(2,1)}, bf16[2,1,2,96,2,768]{5,4,3,2,1,0:T(2,128)(2,1)}, u32[]{:S(2)}, u32[]{:S(2)}) collective-permute-start(bf16[2,1,2,96,2,768]{5,4,3,2,1,0:T(2,128)(2,1)} %add_convert_fusion.7), channel_id=1, source_target_pairs={{0,8},{1,9},{2,10},{3,11},{4,12},{5,13},{6,14},{7,15},{8,0},{9,1},... | collective-permute-start | bytes 3538952 | tf_op jit(solution)/shard_map/ppermute | solution.py:103
  601.8 23.2 %collective-permute-start.14 = (bf16[1,1,2,96,2,576]{5,4,3,2,1,0:T(2,128)(2,1)S(1)}, bf16[1,1,2,96,2,576]{5,4,3,2,1,0:T(2,128)(2,1)S(1)}, u32[]{:S(2)}, u32[]{:S(2)}) collective-permute-start(bf16[1,1,2,96,2,576]{5,4,3,2,1,0:T(2,128)(2,1)S(1)} %add_convert_fusion.12), channel_id=1, source_target_pairs={{0,16},{1,17},{2,18},{3,19},{4,20},{5,21},{6,22},{7,23},{8,24},{9,... | collective-permute-start | bytes 1327112 | tf_op jit(solution)/shard_map/ppermute | solution.py:103
  605.4 50.1 %collective-permute-start.31 = (bf16[2,2,2,96,1,768]{5,3,4,2,1,0:T(8,128)(2,1)}, bf16[2,2,2,96,1,768]{5,3,4,2,1,0:T(8,128)(2,1)}, u32[]{:S(2)}, u32[]{:S(2)}) collective-permute-start(bf16[2,2,2,96,1,768]{5,3,4,2,1,0:T(8,128)(2,1)} %add_convert_fusion.6), channel_id=1, source_target_pairs={{0,2},{1,3},{2,0},{3,1},{4,6},{5,7},{6,4},{7,5},{8,10},{9,11},{10,... | collective-permute-start | bytes 3538952 | tf_op jit(solution)/shard_map/ppermute | solution.py:103
  628.1 14.2 %collective-permute-start.15 = (bf16[1,1,1,96,2,576]{5,4,3,2,1,0:T(2,128)(2,1)}, bf16[1,1,1,96,2,576]{5,4,3,2,1,0:T(2,128)(2,1)}, u32[]{:S(2)}, u32[]{:S(2)}) collective-permute-start(bf16[1,1,1,96,2,576]{5,4,3,2,1,0:T(2,128)(2,1)} %add_convert_fusion.22), channel_id=1, source_target_pairs={{0,4},{1,5},{2,6},{3,7},{4,0},{5,1},{6,2},{7,3},{8,12},{9,13},{10,... | collective-permute-start | bytes 663560 | tf_op jit(solution)/shard_map/ppermute | solution.py:103
  649.5 26.4 %collective-permute-start.39 = (bf16[2,1,1,384,2,192]{3,5,4,2,1,0:T(8,128)(2,1)S(1)}, bf16[2,1,1,384,2,192]{3,5,4,2,1,0:T(8,128)(2,1)S(1)}, u32[]{:S(2)}, u32[]{:S(2)}) collective-permute-start(bf16[2,1,1,384,2,192]{3,5,4,2,1,0:T(8,128)(2,1)S(1)} %add_convert_fusion.9), channel_id=1, source_target_pairs={{0,8},{1,9},{2,10},{3,11},{4,12},{5,13},{6,14},{7,15},{8,0},{9,1},... | collective-permute-start | bytes 1769480 | tf_op jit(solution)/shard_map/ppermute | solution.py:103
  655.2 29.0 %collective-permute-start.26 = (bf16[1,1,2,96,2,768]{5,4,3,2,1,0:T(2,128)(2,1)S(1)}, bf16[1,1,2,96,2,768]{5,4,3,2,1,0:T(2,128)(2,1)S(1)}, u32[]{:S(2)}, u32[]{:S(2)}) collective-permute-start(bf16[1,1,2,96,2,768]{5,4,3,2,1,0:T(2,128)(2,1)S(1)} %add_convert_fusion.11), channel_id=1, source_target_pairs={{0,16},{1,17},{2,18},{3,19},{4,20},{5,21},{6,22},{7,23},{8,24},{9,... | collective-permute-start | bytes 1769480 | tf_op jit(solution)/shard_map/ppermute | solution.py:103
  657.0 15.7 %collective-permute-start.32 = (bf16[2,2,1,96,1,768]{5,3,4,2,1,0:T(8,128)(2,1)S(1)}, bf16[2,2,1,96,1,768]{5,3,4,2,1,0:T(8,128)(2,1)S(1)}, u32[]{:S(2)}, u32[]{:S(2)}) collective-permute-start(bf16[2,2,1,96,1,768]{5,3,4,2,1,0:T(8,128)(2,1)S(1)} %add_convert_fusion.10), channel_id=1, source_target_pairs={{0,4},{1,5},{2,6},{3,7},{4,0},{5,1},{6,2},{7,3},{8,12},{9,13},{10,... | collective-permute-start | bytes 1769480 | tf_op jit(solution)/shard_map/ppermute | solution.py:103
  673.8 15.2 %collective-permute-start.33 = (bf16[2,1,1,96,1,768]{5,3,4,2,1,0:T(8,128)(2,1)S(1)}, bf16[2,1,1,96,1,768]{5,3,4,2,1,0:T(8,128)(2,1)S(1)}, u32[]{:S(2)}, u32[]{:S(2)}) collective-permute-start(bf16[2,1,1,96,1,768]{5,3,4,2,1,0:T(8,128)(2,1)S(1)} %add_convert_fusion.17), channel_id=1, source_target_pairs={{0,8},{1,9},{2,10},{3,11},{4,12},{5,13},{6,14},{7,15},{8,0},{9,1},... | collective-permute-start | bytes 884744 | tf_op jit(solution)/shard_map/ppermute | solution.py:103
  677.0 22.4 %collective-permute-start.40 = (bf16[1,1,1,384,2,192]{3,5,4,2,1,0:T(8,128)(2,1)S(1)}, bf16[1,1,1,384,2,192]{3,5,4,2,1,0:T(8,128)(2,1)S(1)}, u32[]{:S(2)}, u32[]{:S(2)}) collective-permute-start(bf16[1,1,1,384,2,192]{3,5,4,2,1,0:T(8,128)(2,1)S(1)} %add_convert_fusion.16), channel_id=1, source_target_pairs={{0,16},{1,17},{2,18},{3,19},{4,20},{5,21},{6,22},{7,23},{8,24},{9,... | collective-permute-start | bytes 884744 | tf_op jit(solution)/shard_map/ppermute | solution.py:103
  685.9 17.8 %collective-permute-start.27 = (bf16[1,1,1,96,2,768]{5,4,3,2,1,0:T(2,128)(2,1)S(1)}, bf16[1,1,1,96,2,768]{5,4,3,2,1,0:T(2,128)(2,1)S(1)}, u32[]{:S(2)}, u32[]{:S(2)}) collective-permute-start(bf16[1,1,1,96,2,768]{5,4,3,2,1,0:T(2,128)(2,1)S(1)} %add_convert_fusion.20), channel_id=1, source_target_pairs={{0,4},{1,5},{2,6},{3,7},{4,0},{5,1},{6,2},{7,3},{8,12},{9,13},{10,... | collective-permute-start | bytes 884744 | tf_op jit(solution)/shard_map/ppermute | solution.py:103
  690.0 11.6 %collective-permute-start.34 = (bf16[1,1,1,96,1,768]{5,3,4,2,1,0:T(8,128)(2,1)S(1)}, bf16[1,1,1,96,1,768]{5,3,4,2,1,0:T(8,128)(2,1)S(1)}, u32[]{:S(2)}, u32[]{:S(2)}) collective-permute-start(bf16[1,1,1,96,1,768]{5,3,4,2,1,0:T(8,128)(2,1)S(1)} %add_convert_fusion.26), channel_id=1, source_target_pairs={{0,16},{1,17},{2,18},{3,19},{4,20},{5,21},{6,22},{7,23},{8,24},{9,... | collective-permute-start | bytes 442376 | tf_op jit(solution)/shard_map/ppermute | solution.py:103
  700.5 12.1 %collective-permute-start.41 = (bf16[384,384]{0,1:T(8,128)(2,1)S(1)}, bf16[384,384]{0,1:T(8,128)(2,1)S(1)}, u32[]{:S(2)}, u32[]{:S(2)}) collective-permute-start(bf16[384,384]{0,1:T(8,128)(2,1)S(1)} %bitcast.270), channel_id=1, source_target_pairs={{0,2},{1,3},{2,0},{3,1},{4,6},{5,7},{6,4},{7,5},{8,10},{9,11},{10,... | collective-permute-start | bytes 884744 | tf_op jit(solution)/shard_map/ppermute | solution.py:103
  (70 other events, 684.8 us)
